TPU v7x, 32 devices: a whole 2x2x4 slice. The times are simulated.
32 devices in a mesh: grp: 2 (over y), row: 4 (over z), vec: 2 (over x), sub: 2 (over core).
Axes of the slice: x: 2, y: 2, z: 4, core: 2. Of those that a mesh axis runs over, the one named last changes fastest.
Arguments:
- chol_vectors: float32 [64, 1280, 1280], P(('grp', 'vec'), ('row', 'sub')), parts along dimension 0, may hold values from -90 to 90, as said below
- orbitals: float32 [2560, 1280], P(('grp', 'row', 'sub')), parts along dimension 0, may hold values from -0.15625 to 0.15625
- one_body: float32 [2560, 1280], P(('grp', 'row', 'sub')), parts along dimension 0, may hold values from -7.5 to 7.5, as said below
Outputs:
- rotated: float32 [64, 1280, 1280], P(('grp', 'vec'), ('row', 'sub')), parts along dimension 0
- onebody_rot: float32 [2560, 1280], P(('grp', 'row', 'sub')), parts along dimension 0
- diag_mean: float32 [2560], P(('grp', 'row', 'sub')), parts along dimension 0
There are 2 independent parts, one for each index of `grp`. A program takes and returns all parts, laid end to end along the dimension named above; each array names one. Nothing has to cross between parts.
Inputs may be any that keep to these rules, and one draw needn't show every extreme that they name: `chol_vectors`: each vector is a symmetric matrix. `one_body`: a symmetric matrix.
All inputs are finite; a program needn't handle non-finite values.
Results may differ from a plain program's by a relative error of at most 0.00014.
Values sent between devices are 32-bit elements; how exact they have to be, the bound alone decides.
A program may use at most 192 MiB of HBM per device.

v0:
```python
import jax
import jax.numpy as jnp
from jax import lax
from jax.sharding import PartitionSpec as P


def per_device(chol_vectors, orbitals, one_body):
    vec_count = chol_vectors.shape[0]
    row_count = chol_vectors.shape[1]
    highest = lax.Precision.HIGHEST
    full_orb = lax.all_gather(orbitals, ("row", "sub"), axis=0, tiled=True)
    right_rotated = jnp.einsum("gkq,qj->gkj", chol_vectors, full_orb, precision=highest)
    right_onebody = jnp.dot(
        one_body, full_orb, precision=highest, preferred_element_type=jnp.float32
    )
    stacked = jnp.concatenate([right_rotated, right_onebody[None]], axis=0)
    columns = lax.all_to_all(stacked, ("row", "sub"), split_axis=2, concat_axis=1, tiled=True)
    rotated = jnp.einsum("gkj,kp->gjp", columns[:vec_count], full_orb, precision=highest)
    onebody_cols = columns[vec_count]
    onebody_rot = jnp.einsum("kj,kp->jp", onebody_cols, full_orb, precision=highest)
    first_diag = lax.axis_index(("row", "sub")) * row_count
    diag_block = lax.dynamic_slice_in_dim(rotated, first_diag, row_count, 2)
    diag_values = jnp.diagonal(diag_block, axis1=1, axis2=2)
    local_sum = jnp.sum(diag_values * diag_values, axis=0)
    diag_total = lax.psum(local_sum, "vec")
    diag_mean = diag_total / (vec_count * lax.axis_size("vec"))
    return (rotated, onebody_rot, diag_mean)


def solution(mesh):
    in_specs = (
        P(("grp", "vec"), ("row", "sub"), None),
        P(("grp", "row", "sub"), None),
        P(("grp", "row", "sub"), None),
    )
    out_specs = (
        P(("grp", "vec"), ("row", "sub"), None),
        P(("grp", "row", "sub"), None),
        P(("grp", "row", "sub")),
    )
    return jax.shard_map(
        per_device, mesh=mesh, in_specs=in_specs, out_specs=out_specs, check_vma=False
    )
```

profile of v0, /device:TPU:11, one launch (start us, length us, event | category | flops | bytes accessed | tf_op | source)
XLA Modules:
  0.0 790.2 jit_solution(1781603335617103438)
XLA Ops:
  7.2 0.7 all-gather.2.cloned.1.call-update
  7.9 68.0 %all-gather.2.cloned.1.call-done = f32[1280,1280]{1,0:T(8,128)} async-done(((f32[160,1280]{1,0:T(8,128)}), f32[1280,1280]{1,0:T(8,128)}) %all-gather.2.cloned.1.call-update) | async-done | bytes 6553616 | tf_op jit(solution)/shard_map/all_gather | solution.py:11
  75.9 6.7 convolution_bitcast_fusion
  82.6 76.4 %fusion.2 = f32[16,160,1280]{2,1,0:T(8,128)} fusion(f32[16,160,1280]{2,1,0:T(8,128)} %param.3, f32[1280,1280]{1,0:T(8,128)} %all-gather.2.cloned.1.call-done), kind=kOutput, calls=%fused_computation.5 | convolution fusion | flops 50331648000 | bytes 32768000 | tf_op jit(solution)/shard_map/gkq,qj->gkj/dot_general | solution.py:12
  159.0 11.0 %pad_maximum_fusion = f32[17,160,1280]{2,1,0:T(8,128)} fusion(f32[1,160,1280]{2,1,0:T(8,128)S(1)} %convolution_bitcast_fusion, f32[16,160,1280]{2,1,0:T(8,128)} %fusion.2), kind=kLoop, calls=%fused_computation.2 | loop fusion | flops 3481600 | bytes 27852800 | tf_op jit(solution)/shard_map/concatenate | solution.py:16
  170.0 27.3 %copy.10 = f32[17,160,1280]{1,0,2:T(8,128)} copy(f32[17,160,1280]{2,1,0:T(8,128)} %pad_maximum_fusion) | data formatting | bytes 27852800 | tf_op jit(solution)/shard_map/concatenate | solution.py:16
  197.3 30.2 %reshape.16 = f32[8,1,435200]{2,1,0:T(1,128)} reshape(f32[1280,17,160]{2,1,0:T(8,128)} %bitcast.28) | data formatting | bytes 27852800
  227.5 8.3 %all-to-all-start = ((f32[8,1,435200]{2,1,0:T(1,128)}), f32[8,1,435200]{2,1,0:T(1,128)}, u32[]{:S(2)}, u32[]{:S(2)}) async-start(f32[8,1,435200]{2,1,0:T(1,128)} %reshape.16), calls=%async_computation | async-start | bytes 27852800 | tf_op jit(solution)/shard_map/all_to_all | solution.py:17
  235.8 298.9 %all-to-all-done = f32[8,1,435200]{2,1,0:T(1,128)} async-done(((f32[8,1,435200]{2,1,0:T(1,128)}), f32[8,1,435200]{2,1,0:T(1,128)}, u32[]{:S(2)}, u32[]{:S(2)}) %all-to-all-start) | async-done | bytes 13926432 | tf_op jit(solution)/shard_map/all_to_all | solution.py:17
  534.7 0.5 broadcast.22
  535.2 78.9 %reduce.1 = f32[8,435200]{1,0:T(8,128)} reduce(f32[8,1,435200]{2,1,0:T(1,128)} %all-to-all-done, f32[]{:T(128)} %broadcast.22), dimensions={1}, to_apply=%all_to_all.11.reduce_sub_computation | reduce | bytes 27852804 | tf_op jit(solution)/shard_map/all_to_all | solution.py:17
  614.1 31.9 %reshape.17 = f32[1280,17,160]{2,1,0:T(8,128)} reshape(f32[8,435200]{1,0:T(8,128)} %reduce.1) | data formatting | bytes 27852800
  646.0 20.1 %copy.14 = f32[17,160,8,160]{1,2,3,0:T(8,128)S(1)} copy(f32[17,160,8,160]{1,0,3,2:T(8,128)} %bitcast.29) | data formatting | bytes 27852800 | tf_op jit(solution)/shard_map/all_to_all | solution.py:17
  666.2 7.5 slice.15
  673.7 19.8 %slice.11 = f32[16,1280,160]{1,2,0:T(8,128)} reshape(f32[16,8,160,160]{2,1,3,0:T(8,128)} %slice.15) | data formatting | bytes 26214400 | tf_op jit(solution)/shard_map/slice | solution.py:18
  693.5 1.5 squeeze.3
  695.0 57.4 %fusion = f32[16,160,1280]{2,1,0:T(8,128)S(1)} fusion(f32[16,1280,160]{1,2,0:T(8,128)} %slice.11, f32[1280,1280]{1,0:T(8,128)} %all-gather.2.cloned.1.call-done), kind=kOutput, calls=%fused_computation.3 | convolution fusion | flops 50331648000 | bytes 32768000 | tf_op jit(solution)/shard_map/gkj,kp->gjp/dot_general | solution.py:18
  752.4 4.9 copy-done.2
  757.3 0.7 constant_dynamic-slice_fusion
  758.1 7.1 copy.12
  765.1 5.6 gather_fusion
  770.8 3.8 psum.7
  774.6 0.6 broadcast_multiply_fusion
  775.2 7.9 %fusion.4 = f32[160,1280]{1,0:T(8,128)} fusion(f32[1280,160]{0,1:T(8,128)} %squeeze.3, f32[1280,1280]{1,0:T(8,128)} %all-gather.2.cloned.1.call-done), kind=kOutput, calls=%fused_computation.12 | convolution fusion | flops 3145728000 | bytes 8192000 | tf_op jit(solution)/shard_map/kj,kp->jp/dot_general | solution.py:20
  (9 shorter events, 0.3 us)
Async XLA Ops:
  7.2 68.7 %copy-start = (f32[160,1280]{1,0:T(8,128)S(1)}, f32[160,1280]{1,0:T(8,128)}, u32[]{:S(2)}) copy-start(f32[160,1280]{1,0:T(8,128)} %param.5) | copy-start | bytes 2457604
  7.2 68.7 %all-gather.2.cloned.1.call-start = ((), (), s32[]{:S(2)}) async-start(), calls=%async_computation.1 | async-start | bytes 7372800 | tf_op jit(solution)/shard_map/all_gather | solution.py:11
  227.5 307.2 %all-to-all-start = ((f32[8,1,435200]{2,1,0:T(1,128)}), f32[8,1,435200]{2,1,0:T(1,128)}, u32[]{:S(2)}, u32[]{:S(2)}) async-start(f32[8,1,435200]{2,1,0:T(1,128)} %reshape.16), calls=%async_computation | async-start | bytes 27852800 | tf_op jit(solution)/shard_map/all_to_all | solution.py:17
  752.4 5.0 copy-start.2
  757.3 25.8 %copy-start.1 = (f32[160,1280]{1,0:T(8,128)S(1)}, f32[160,1280]{1,0:T(8,128)}, u32[]{:S(2)}) copy-start(f32[160,1280]{1,0:T(8,128)} %param.5) | copy-start | bytes 2457604
Sparse Core Ops, SparseCore 0:
  9.7 66.1 all-gather.1
where the time goes:
time: 800 us; the launch traced here: 790 us
  waiting for transfers between devices  368 us (46%)
  local copies, waits for them, and re-layouts  157 us (20%)
  matrix products  148 us (18%)
  other arithmetic  90.6 us (11%)
  between operations  14.3 us (2%)
  starting transfers between devices  8.32 us (1%)
    all_to_all x1, waiting for transfers between devices, per_device(): lax.all_to_all(stacked, ('row', 'sub'), split_axis=2, concat_axis=1, tile...  299 us
    all_to_all x1, other arithmetic, per_device(): lax.all_to_all(stacked, ('row', 'sub'), split_axis=2, concat_axis=1, tile...  78.9 us
    dot_general x1, matrix products, per_device(): jnp.einsum('gkq,qj->gkj', chol_vectors, full_orb, precision=highest)  76.4 us
    all_gather x1, waiting for transfers between devices, per_device(): full_orb = lax.all_gather(orbitals, ('row', 'sub'), axis=0, tiled=True)  68 us
    unnamed x8, local copies, waits for them, and re-layouts  67 us
    dot_general x1, matrix products, per_device(): jnp.einsum('gkj,kp->gjp', columns[:vec_count], full_orb, precision=highest)  57.4 us
    concatenate x1, local copies, waits for them, and re-layouts, per_device(): stacked = jnp.concatenate([right_rotated, right_onebody[None]], axis=0)  27.3 us
    slice x2, local copies, waits for them, and re-layouts, per_device(): columns[:vec_count]  27.3 us
  transfers between devices with their start and end apart: 2, of which 2 were waited for; matrix products, arithmetic and copies ran while one was open for 0% of the time, Pallas kernels for 0%

commit v1 on v0

v1 whole, which is shorter than its diff:
```python
import functools

import jax
import jax.numpy as jnp
from jax import lax
from jax.experimental import pallas as pl
from jax.experimental.pallas import tpu as pltpu
from jax.sharding import PartitionSpec as P

NT = (((1,), (1,)), ((), ()))
NN = (((1,), (0,)), ((), ()))


def split(value):
    high = value.astype(jnp.bfloat16)
    low = (value - high.astype(jnp.float32)).astype(jnp.bfloat16)
    return high, low


def dot3(a_high, a_low, b_high, b_low, dims):
    dot = functools.partial(
        lax.dot_general, dimension_numbers=dims, preferred_element_type=jnp.float32
    )
    return dot(a_high, b_high) + (dot(a_high, b_low) + dot(a_low, b_high))


def rotate_kernel(
    rows, subs, chol, hbody, coef, coef_t, rotated, onebody, diag,
    c_high, c_low, t_high, t_low, slot, x_high, x_low, out_buf,
    send, recv, h_send, h_recv,
    load_sem, store_sem, send_sem, recv_sem, h_send_sem, h_recv_sem,
):
    chunks, group, block, width = chol.shape
    n = rows * subs
    lanes = group * block
    h_lanes = h_send.shape[2]
    pieces = width // lanes
    row = lax.axis_index("row")
    sub = lax.axis_index("sub")
    me = row * subs + sub

    def place(index):
        return {"row": index // subs, "sub": lax.rem(index, subs)}

    barrier = pltpu.get_barrier_semaphore()

    def greet(step, carry):
        pl.semaphore_signal(
            barrier, inc=1, device_id=place(lax.rem(me + step, n)),
            device_id_type=pl.DeviceIdType.MESH,
        )
        return carry

    lax.fori_loop(1, n, greet, 0)

    def load(source):
        return pltpu.make_async_copy(source, slot, load_sem)

    for piece in range(pieces):
        copy = load(coef.at[piece])
        copy.start()
        copy.wait()
        for g in range(group):
            high, low = split(slot[g])
            at = pl.ds(piece * lanes + g * block, block)
            c_high[at, :] = high
            c_low[at, :] = low
    per = rows // pieces
    for piece in range(pieces):
        copy = load(coef_t.at[piece])
        copy.start()
        copy.wait()
        for r in range(per):
            part = slot[pl.ds(r * subs, subs)].reshape(subs * block, width)
            high, low = split(part)
            t_high[piece * per + r] = high
            t_low[piece * per + r] = low
    load(chol.at[0]).start()
    pl.semaphore_wait(barrier, n - 1)

    def message(c, index, mine):
        return pltpu.make_async_remote_copy(
            src_ref=send.at[c, index],
            dst_ref=recv.at[c, mine],
            send_sem=send_sem.at[c, index],
            recv_sem=recv_sem.at[c, mine],
            device_id=place(index),
            device_id_type=pl.DeviceIdType.MESH,
        )

    def h_message(index, mine):
        return pltpu.make_async_remote_copy(
            src_ref=h_send.at[index],
            dst_ref=h_recv.at[mine],
            send_sem=h_send_sem.at[index],
            recv_sem=h_recv_sem.at[mine],
            device_id=place(index),
            device_id_type=pl.DeviceIdType.MESH,
        )

    rest = jnp.zeros((h_lanes - block, width), jnp.float32)
    high = jnp.concatenate([hbody[...], rest], axis=0)
    high, low = split(high)
    x_high[pl.ds(0, h_lanes), :] = high
    x_low[pl.ds(0, h_lanes), :] = low

    def h_dest(step, carry):
        to_row = lax.rem(row + rows // 2 + step, rows)
        half = dot3(
            t_high[to_row], t_low[to_row],
            x_high[pl.ds(0, h_lanes), :], x_low[pl.ds(0, h_lanes), :], NT,
        )
        for s in range(subs):
            index = to_row * subs + s
            part = half[s * block:(s + 1) * block]

            @pl.when(index != me)
            def _():
                h_send[index] = part
                h_message(index, me).start()

            @pl.when(index == me)
            def _():
                h_recv[me] = part

        return carry

    lax.fori_loop(0, rows, h_dest, 0)

    def first_stage(c, carry):
        load(chol.at[c]).wait()
        for g in range(group):
            high, low = split(slot[g])
            at = pl.ds(g * block, block)
            if block % 16 == 0:
                x_high[at, :] = high
                x_low[at, :] = low
        if block % 16:
            high, low = split(slot[...].reshape(lanes, width))
            x_high[...] = high
            x_low[...] = low

        @pl.when(c + 1 < chunks)
        def _():
            load(chol.at[c + 1]).start()

        def dest(step, inner):
            to_row = lax.rem(row + rows // 2 + step, rows)
            half = dot3(t_high[to_row], t_low[to_row], x_high[...], x_low[...], NT)
            for s in range(subs):
                index = to_row * subs + s
                part = half[s * block:(s + 1) * block]

                @pl.when(index != me)
                def _():
                    send[c, index] = part
                    message(c, index, me).start()

                @pl.when(index == me)
                def _():
                    recv[c, me] = part

            return inner

        lax.fori_loop(0, rows, dest, 0)
        return carry

    lax.fori_loop(0, chunks, first_stage, 0)

    def h_arrive(step, carry):
        index = lax.rem(me + step, n)
        h_message(index, index).wait_recv()
        return carry

    lax.fori_loop(1, n, h_arrive, 0)
    for k in range(n):
        slot[0, :, k * block:(k + 1) * block] = h_recv[k, :, :block]
    high, low = split(slot[0])
    tile = 256
    for t in range(width // tile):
        at = pl.ds(t * tile, tile)
        onebody[:, at] = dot3(high, low, c_high[:, at], c_low[:, at], NN)

    diag[...] = jnp.zeros_like(diag)

    def second_stage(c, carry):
        def arrive(step, inner):
            index = lax.rem(me + step, n)
            message(c, index, index).wait_recv()
            return inner

        lax.fori_loop(1, n, arrive, 0)
        for g in range(group):
            for k in range(n):
                slot[g, :, k * block:(k + 1) * block] = (
                    recv[c, k, :, g * block:(g + 1) * block]
                )
        for g in range(group):
            high, low = split(slot[g])
            at = pl.ds(g * block, block)
            if block % 16 == 0:
                x_high[at, :] = high
                x_low[at, :] = low
        if block % 16:
            high, low = split(slot[...].reshape(lanes, width))
            x_high[...] = high
            x_low[...] = low

        def columns(t, inner):
            at = pl.ds(pl.multiple_of(t * tile, tile), tile)
            result = dot3(x_high[...], x_low[...], c_high[:, at], c_low[:, at], NN)
            out_buf[:, :, at] = result.reshape(group, block, tile)
            return inner

        lax.fori_loop(0, width // tile, columns, 0)
        copy = pltpu.make_async_copy(out_buf, rotated.at[c], store_sem)
        copy.start()
        own = (
            lax.broadcasted_iota(jnp.int32, (block, width), 1)
            == lax.broadcasted_iota(jnp.int32, (block, width), 0) + me * block
        )
        for g in range(group):
            picked = jnp.sum(jnp.where(own, out_buf[g], 0.0), axis=1, keepdims=True)
            diag[...] += jnp.broadcast_to(picked * picked, diag.shape)
        copy.wait()
        return carry

    lax.fori_loop(0, chunks, second_stage, 0)

    def drain(step, carry):
        index = lax.rem(me + step, n)
        h_message(index, me).wait_send()

        def each(c, inner):
            message(c, index, me).wait_send()
            return inner

        return lax.fori_loop(0, chunks, each, carry)

    lax.fori_loop(1, n, drain, 0)


def per_device(rows, subs, chol_vectors, orbitals, one_body):
    count, block, width = chol_vectors.shape
    n = rows * subs
    group = 1
    while (group * block) % 128 or count % group:
        group += 1
    lanes = group * block
    chunks = count // group
    pieces = width // lanes
    h_lanes = -(-block // 128) * 128
    full_orb = lax.all_gather(orbitals, ("row", "sub"), axis=0, tiled=True)
    coef = full_orb.reshape(pieces, group, block, width)
    coef_t = full_orb.T.reshape(pieces, group, block, width)
    flops = 2 * 6 * (count + 1) * block * width * width
    hbm = pl.BlockSpec(memory_space=pl.ANY)
    vmem = pl.BlockSpec(memory_space=pltpu.VMEM)
    bf16, f32 = jnp.bfloat16, jnp.float32
    rotated, onebody, diag = pl.pallas_call(
        functools.partial(rotate_kernel, rows, subs),
        out_shape=(
            jax.ShapeDtypeStruct((chunks, group, block, width), f32),
            jax.ShapeDtypeStruct((block, width), f32),
            jax.ShapeDtypeStruct((block, 128), f32),
        ),
        in_specs=[hbm, vmem, hbm, hbm],
        out_specs=(hbm, vmem, vmem),
        scratch_shapes=[
            pltpu.VMEM((width, width), bf16),
            pltpu.VMEM((width, width), bf16),
            pltpu.VMEM((rows, subs * block, width), bf16),
            pltpu.VMEM((rows, subs * block, width), bf16),
            pltpu.VMEM((group, block, width), f32),
            pltpu.VMEM((lanes, width), bf16),
            pltpu.VMEM((lanes, width), bf16),
            pltpu.VMEM((group, block, width), f32),
            pltpu.VMEM((chunks, n, block, lanes), f32),
            pltpu.VMEM((chunks, n, block, lanes), f32),
            pltpu.VMEM((n, block, h_lanes), f32),
            pltpu.VMEM((n, block, h_lanes), f32),
            pltpu.SemaphoreType.DMA,
            pltpu.SemaphoreType.DMA,
            pltpu.SemaphoreType.DMA((chunks, n)),
            pltpu.SemaphoreType.DMA((chunks, n)),
            pltpu.SemaphoreType.DMA((n,)),
            pltpu.SemaphoreType.DMA((n,)),
        ],
        compiler_params=pltpu.CompilerParams(
            collective_id=0, has_side_effects=True,
            vmem_limit_bytes=62 * 1024 * 1024,
        ),
        cost_estimate=pl.CostEstimate(
            flops=flops, bytes_accessed=8 * count * block * width, transcendentals=0
        ),
    )(chol_vectors.reshape(chunks, group, block, width), one_body, coef, coef_t)
    diag_total = lax.psum(diag[:, 0], "vec")
    diag_mean = diag_total / (count * lax.axis_size("vec"))
    return rotated.reshape(count, block, width), onebody, diag_mean


def solution(mesh):
    in_specs = (
        P(("grp", "vec"), ("row", "sub"), None),
        P(("grp", "row", "sub"), None),
        P(("grp", "row", "sub"), None),
    )
    out_specs = (
        P(("grp", "vec"), ("row", "sub"), None),
        P(("grp", "row", "sub"), None),
        P(("grp", "row", "sub")),
    )
    return jax.shard_map(
        functools.partial(per_device, mesh.shape["row"], mesh.shape["sub"]),
        mesh=mesh, in_specs=in_specs, out_specs=out_specs, check_vma=False,
    )
```

time: 800 us -> 444 us (0.56); the launches traced: 790 us -> 444 us
  Pallas kernels: 0 us -> 336 us
  waiting for transfers between devices: 368 us -> 68.7 us
  matrix products: 148 us -> 0 us
  local copies, waits for them, and re-layouts: 157 us -> 21 us
  other arithmetic: 90.6 us -> 0.57 us
  starting transfers between devices: 8.32 us -> 0.04 us
    pallas_call x0 -> x1, Pallas kernels: none -> 336 us  [per_device(): pl.pallas_call(functools.partial(rotate_kernel, rows, subs), out_shape=(j...]
    all_to_all x1 -> x0, waiting for transfers between devices: 299 us -> none  [per_device(): lax.all_to_all(stacked, ('row', 'sub'), split_axis=2, concat_axis=1, tile...]
    dot_general x4 -> x0, matrix products: 148 us -> none  [the longest x1 76.4 us: per_device(): jnp.einsum('gkq,qj->gkj', chol_vectors, full_orb, precision=highest)]
    all_to_all x1 -> x0, other arithmetic: 78.9 us -> none  [per_device(): lax.all_to_all(stacked, ('row', 'sub'), split_axis=2, concat_axis=1, tile...]
    unnamed x8 -> x4, local copies, waits for them, and re-layouts: 67 us -> 11.9 us
    concatenate x1 -> x0, local copies, waits for them, and re-layouts: 27.3 us -> none  [per_device(): stacked = jnp.concatenate([right_rotated, right_onebody[None]], axis=0)]
    slice x3 -> x1, local copies, waits for them, and re-layouts: 27.4 us -> 0.99 us  [per_device(): diag_total = lax.psum(diag[:, 0], 'vec')]
    all_to_all x2 -> x0, local copies, waits for them, and re-layouts: 20.6 us -> none  [per_device(): lax.all_to_all(stacked, ('row', 'sub'), split_axis=2, concat_axis=1, tile...]
  transfers between devices with their start and end apart: 2 -> 1, of which waited for: 2 -> 1; matrix products, arithmetic and copies ran while one was open for 0% -> 0% of each run, Pallas kernels for 0% -> 0%
where the time goes in v1:
time: 444 us
  Pallas kernels  336 us (76%)
  waiting for transfers between devices  68.7 us (15%)
  local copies, waits for them, and re-layouts  21 us (5%)
  between operations  14 us (3%)
    pallas_call x1, Pallas kernels, per_device(): pl.pallas_call(functools.partial(rotate_kernel, rows, subs), out_shape=(j...  336 us
    all_gather x1, waiting for transfers between devices, per_device(): full_orb = lax.all_gather(orbitals, ('row', 'sub'), axis=0, tiled=True)  68 us
    unnamed x4, local copies, waits for them, and re-layouts  11.9 us
  transfers between devices with their start and end apart: 1, of which 1 were waited for; matrix products, arithmetic and copies ran while one was open for 0% of the time, Pallas kernels for 0%

profile of v1, /device:TPU:11, one launch (start us, length us, event | category | flops | bytes accessed | tf_op | source)
XLA Modules:
  0.0 443.9 jit_solution(10312323797768401908)
XLA Ops:
  7.2 0.0 all-gather.2.cloned.1.call-start
  7.2 0.7 all-gather.2.cloned.1.call-update
  7.9 68.0 %all-gather.2.cloned.1.call-done = f32[1280,1280]{1,0:T(8,128)} async-done(((f32[160,1280]{1,0:T(8,128)}), f32[1280,1280]{1,0:T(8,128)}) %all-gather.2.cloned.1.call-update) | async-done | bytes 6553616 | tf_op jit(solution)/shard_map/all_gather | solution.py:253
  75.9 8.1 %copy.7 = f32[1280,1280]{1,0:T(8,128)} copy(f32[1280,1280]{0,1:T(8,128)} %bitcast.6) | data formatting | bytes 13107200 | tf_op jit(solution)/shard_map/transpose | solution.py:255
  84.0 335.7 %shard_map.58 = (f32[4,4,160,1280]{3,2,1,0:T(8,128)}, f32[160,1280]{1,0:T(8,128)}, f32[160,128]{1,0:T(8,128)}) custom-call(f32[4,4,160,1280]{3,2,1,0:T(8,128)} %bitcast.9, f32[160,1280]{1,0:T(8,128)} %hbody.1, f32[2,4,160,1280]{3,2,1,0:T(8,128)} %bitcast.7, f32[2,4,160,1280]{3,2,1,0:T(8,128)} %bitcast.8), custom_call_target="tpu_custom_call" | custom-call | flops 53477376000 | bytes 26214400 | tf_op jit(solution)/shard_map/pallas_call | solution.py:260
  419.7 1.0 slice_reduce_fusion
  420.7 3.8 psum.7
  424.5 0.6 broadcast_multiply_fusion
  425.1 0.0 copy-start
  425.1 11.0 %copy.10 = f32[16,160,1280]{2,1,0:T(8,128)} copy(f32[16,160,1280]{2,1,0:T(8,128)} %bitcast.5) | data formatting | bytes 26214400
  436.2 0.0 copy-done
  436.2 0.9 copy.11
Async XLA Ops:
  7.2 68.7 %all-gather.2.cloned.1.call-start = ((), (), s32[]{:S(2)}) async-start(), calls=%async_computation | async-start | bytes 7372800 | tf_op jit(solution)/shard_map/all_gather | solution.py:253
  425.1 11.0 %copy-start = (f32[160,1280]{1,0:T(8,128)S(1)}, f32[160,1280]{1,0:T(8,128)}, u32[]{:S(2)}) copy-start(f32[160,1280]{1,0:T(8,128)} %get-tuple-element.13) | copy-start | bytes 2457604
Sparse Core Ops, SparseCore 0:
  9.6 66.1 all-gather.1

commit v2 on v1

--- a/solution.py
+++ b/solution.py
@@ -250,7 +250,9 @@
     chunks = count // group
     pieces = width // lanes
     h_lanes = -(-block // 128) * 128
-    full_orb = lax.all_gather(orbitals, ("row", "sub"), axis=0, tiled=True)
+    share = block // lax.axis_size("vec")
+    own = lax.dynamic_slice_in_dim(orbitals, lax.axis_index("vec") * share, share, 0)
+    full_orb = lax.all_gather(own, ("row", "sub", "vec"), axis=0, tiled=True)
     coef = full_orb.reshape(pieces, group, block, width)
     coef_t = full_orb.T.reshape(pieces, group, block, width)
     flops = 2 * 6 * (count + 1) * block * width * width

time: 444 us -> 443 us (level)
    unnamed x4 -> x6, local copies, waits for them, and re-layouts: 11.9 us -> 13 us
where the time goes in v2:
time: 443 us; the launch traced here: 442 us
  Pallas kernels  335 us (76%)
  waiting for transfers between devices  65.8 us (15%)
  local copies, waits for them, and re-layouts  22.9 us (5%)
  between operations  14.1 us (3%)
    pallas_call x1, Pallas kernels, per_device(): pl.pallas_call(functools.partial(rotate_kernel, rows, subs), out_shape=(j...  335 us
    all_gather x1, waiting for transfers between devices, per_device(): full_orb = lax.all_gather(own, ('row', 'sub', 'vec'), axis=0, tiled=True)  65.8 us
    unnamed x6, local copies, waits for them, and re-layouts  13 us
  transfers between devices with their start and end apart: 1, of which 1 were waited for; matrix products, arithmetic and copies ran while one was open for 0% of the time, Pallas kernels for 0%

profile of v2, /device:TPU:11, one launch (start us, length us, event | category | flops | bytes accessed | tf_op | source)
XLA Modules:
  0.0 441.7 jit_solution(4093220877726277134)
XLA Ops:
  7.2 0.0 copy-start
  7.2 0.0 all-gather.2.cloned.1.call-start
  7.2 1.1 copy-done
  8.3 0.8 constant_dynamic-slice_fusion
  9.1 0.0 all-gather.2.cloned.1.call-update
  9.1 65.8 %all-gather.2.cloned.1.call-done = f32[1280,1280]{1,0:T(8,128)} async-done(((f32[80,1280]{1,0:T(8,128)}), f32[1280,1280]{1,0:T(8,128)}) %all-gather.2.cloned.1.call-update) | async-done | bytes 6553616 | tf_op jit(solution)/shard_map/all_gather | solution.py:255
  74.9 8.1 %copy.7 = f32[1280,1280]{1,0:T(8,128)} copy(f32[1280,1280]{0,1:T(8,128)} %bitcast.6) | data formatting | bytes 13107200 | tf_op jit(solution)/shard_map/transpose | solution.py:257
  83.0 334.5 %shard_map.58 = (f32[4,4,160,1280]{3,2,1,0:T(8,128)}, f32[160,1280]{1,0:T(8,128)}, f32[160,128]{1,0:T(8,128)}) custom-call(f32[4,4,160,1280]{3,2,1,0:T(8,128)} %bitcast.9, f32[160,1280]{1,0:T(8,128)} %hbody.1, f32[2,4,160,1280]{3,2,1,0:T(8,128)} %bitcast.7, f32[2,4,160,1280]{3,2,1,0:T(8,128)} %bitcast.8), custom_call_target="tpu_custom_call" | custom-call | flops 53477376000 | bytes 26214400 | tf_op jit(solution)/shard_map/pallas_call | solution.py:262
  417.5 1.0 slice_reduce_fusion
  418.5 3.8 psum.7
  422.3 0.6 broadcast_multiply_fusion
  422.9 0.0 copy-start.1
  422.9 11.0 %copy.10 = f32[16,160,1280]{2,1,0:T(8,128)} copy(f32[16,160,1280]{2,1,0:T(8,128)} %bitcast.5) | data formatting | bytes 26214400
  433.9 0.0 copy-done.1
  433.9 0.9 copy.11
Async XLA Ops:
  7.2 1.2 copy-start
  7.2 67.7 %all-gather.2.cloned.1.call-start = ((), (), s32[]{:S(2)}) async-start(), calls=%async_computation | async-start | bytes 6963200 | tf_op jit(solution)/shard_map/all_gather | solution.py:255
  422.9 11.0 %copy-start.1 = (f32[160,1280]{1,0:T(8,128)S(1)}, f32[160,1280]{1,0:T(8,128)}, u32[]{:S(2)}) copy-start(f32[160,1280]{1,0:T(8,128)} %get-tuple-element.13) | copy-start | bytes 2457604
Sparse Core Ops, SparseCore 0:
  10.9 63.9 all-gather.1
